TPU v7x, 32 devices: a whole 2x2x4 slice. The times are simulated.
32 devices in a mesh: dp: 8 (over z, x), tensor: 4 (over y, core).
Axes of the slice: x: 2, y: 2, z: 4, core: 2. Of those that a mesh axis runs over, the one named last changes fastest.
Arguments:
- tokens_in: bfloat16 [12288, 768], P('dp'), may hold values from -6 to 6
- cotangent: bfloat16 [12288, 768], P('dp'), may hold values from -6 to 6
- span_mask: int32 [12288], P('dp'), may hold values from 0 to 1, as said below
- lengths: int32 [24], P('dp'), may hold values from 128 to 512, as said below
- step: int32 [1], replicated, may hold values from 1000 to 31999
- warmup: int32 [1], replicated, may hold values from 1000 to 29999
- total: int32 [1], replicated, may hold values from 32000 to 40000
- w_qkv: float32 [768, 3, 768], P(None, None, 'tensor'), may hold values from -0.21875 to 0.21875
- w_out: float32 [768, 768], P(None, 'tensor'), may hold values from -1.25 to 1.25
- w_in: float32 [768, 3072], P(None, 'tensor'), may hold values from -0.21875 to 0.21875
- w_back: float32 [768, 3072], P(None, 'tensor'), may hold values from -0.109375 to 0.109375
- gains: float32 [2, 768], replicated, may hold values from 0.5 to 1.5
- biases: float32 [6, 768], replicated, may hold values from -3 to 3
- bias_in: float32 [3072], replicated, may hold values from -3 to 3
- mom_qkv: float32 [2, 768, 3, 768], P(None, 'dp', None, 'tensor'), as said below
- mom_out: float32 [2, 768, 768], P(None, 'dp', 'tensor'), as said below
- mom_in: float32 [2, 768, 3072], P(None, 'dp', 'tensor'), as said below
- mom_back: float32 [2, 768, 3072], P(None, 'dp', 'tensor'), as said below
- mom_gains: float32 [2, 2, 768], replicated, as said below
- mom_biases: float32 [2, 6, 768], replicated, as said below
- mom_bias_in: float32 [2, 3072], replicated, as said below
Outputs:
- normed_out: bfloat16 [12288, 768], P('dp')
- input_grad: float32 [12288, 768], P('dp')
- change_qkv: float32 [768, 3, 768], P(None, None, 'tensor')
- change_out_proj: float32 [768, 768], P(None, 'tensor')
- change_in_proj: float32 [768, 3072], P(None, 'tensor')
- change_back_proj: float32 [768, 3072], P(None, 'tensor')
- change_gains: float32 [2, 768], replicated
- change_biases: float32 [6, 768], replicated
- change_bias_in: float32 [3072], replicated
- new_mom_qkv: float32 [2, 768, 3, 768], P(None, 'dp', None, 'tensor')
- new_mom_out: float32 [2, 768, 768], P(None, 'dp', 'tensor')
- new_mom_in: float32 [2, 768, 3072], P(None, 'dp', 'tensor')
- new_mom_back: float32 [2, 768, 3072], P(None, 'dp', 'tensor')
- new_mom_gains: float32 [2, 2, 768], replicated
- new_mom_biases: float32 [2, 6, 768], replicated
- new_mom_bias_in: float32 [2, 3072], replicated
Inputs may be any that keep to these rules, and one draw needn't show every extreme that they name: `span_mask`: marked positions lie below their sequence's length and form unions of spans of 1 to 10 positions; each sequence has at most 76 of them, and in every draw each of the 3 sequences of some index of dp has exactly 76. `lengths`: a sequence's real tokens stand at its start, the rest is padding. step < total. warmup < total. `mom_qkv`: index 1 of the leading dimension holds positive second moments. `mom_out`: index 1 of the leading dimension holds positive second moments. `mom_in`: index 1 of the leading dimension holds positive second moments. `mom_back`: index 1 of the leading dimension holds positive second moments. `mom_gains`: index 1 of the leading dimension holds positive second moments. `mom_biases`: index 1 of the leading dimension holds positive second moments. `mom_bias_in`: index 1 of the leading dimension holds positive second moments.
All inputs are finite; a program needn't handle non-finite values.
Results may differ from a plain program's by a relative error of at most 0.017.
The roundings to bfloat16 on the way count: a program that leaves them out, or rounds other values in their place, can miss the bound.
Values sent between devices are 32-bit elements; how exact they have to be, the bound alone decides.
A program may use at most 128 MiB of HBM per device.

v0:
```python
import math
import jax
import jax.numpy as jnp
from jax import lax
from jax.sharding import PartitionSpec as P

HD = 64
SPAN_ROWS = 80
NORM_EPS = 1e-12
BETA_ONE = 0.9
BETA_TWO = 0.999
ADAM_EPS = 1e-06
WEIGHT_DECAY = 0.01


def layer_norm(values, gain, shift):
    center = values - jnp.mean(values, axis=-1, keepdims=True)
    spread = jnp.mean(center * center, axis=-1, keepdims=True)
    return center * lax.rsqrt(spread + NORM_EPS) * gain + shift


def exact_gelu(values):
    return jax.nn.gelu(values, approximate=False)


def outer_sum(left, right):
    return jnp.einsum("ta,tb->ab", left, right, preferred_element_type=jnp.float32)


def adam_step(weight, grad, moments, ratio, corr_one, corr_two, decay):
    first = BETA_ONE * moments[0] + (1.0 - BETA_ONE) * grad
    second = BETA_TWO * moments[1] + (1.0 - BETA_TWO) * grad * grad
    update = first / corr_one / (jnp.sqrt(second / corr_two) + ADAM_EPS) + decay * weight
    return (-ratio * update, jnp.stack([first, second]))


def on_device(
    tokens_in,
    cotangent,
    span_mask,
    lengths,
    step,
    warmup,
    total,
    w_qkv,
    w_out,
    w_in,
    w_back,
    gains,
    biases,
    bias_in,
    mom_qkv,
    mom_out,
    mom_in,
    mom_back,
    mom_gains,
    mom_biases,
    mom_bias_in,
):
    row_count, model_width = tokens_in.shape
    seq_count = lengths.shape[0]
    seq_length = row_count // seq_count
    head_cols = w_qkv.shape[2]
    hidden_cols = w_in.shape[1]
    head_size = HD
    local_heads = head_cols // head_size
    query_scale = 1.0 / math.sqrt(head_size)
    tensor_slot = lax.axis_index("tensor")
    bias_query = lax.dynamic_slice_in_dim(biases[0], tensor_slot * head_cols, head_cols)
    bias_value = lax.dynamic_slice_in_dim(biases[1], tensor_slot * head_cols, head_cols)
    bias_hidden = lax.dynamic_slice_in_dim(bias_in, tensor_slot * hidden_cols, hidden_cols)
    qkv_low = w_qkv.astype(jnp.bfloat16).reshape(model_width, 3 * head_cols)
    out_low = w_out.astype(jnp.bfloat16)
    in_low = w_in.astype(jnp.bfloat16)
    down_low = w_back.astype(jnp.bfloat16)
    projected = jnp.dot(tokens_in, qkv_low, preferred_element_type=jnp.float32).reshape(
        row_count, 3, head_cols
    )
    attn_shape = (seq_count, seq_length, local_heads, head_size)
    queries = (
        ((projected[:, 0] + bias_query) * query_scale).astype(jnp.bfloat16).reshape(attn_shape)
    )
    keys = projected[:, 1].astype(jnp.bfloat16).reshape(attn_shape)
    values = (projected[:, 2] + bias_value).astype(jnp.bfloat16).reshape(attn_shape)
    positions = jnp.arange(seq_length, dtype=jnp.int32)
    inside = positions[None, :] < lengths[:, None]
    key_bias = jnp.where(inside, 0.0, -1000000000.0).astype(jnp.float32)

    def score_block():
        raw = jnp.einsum("sqhd,skhd->shqk", queries, keys, preferred_element_type=jnp.float32)
        return raw + key_bias[:, None, None, :]

    scores = score_block()
    peak = jnp.max(scores, axis=-1, keepdims=True)
    log_total = peak + jnp.log(jnp.sum(jnp.exp(scores - peak), axis=-1, keepdims=True))
    probs_low = jnp.exp(scores - log_total).astype(jnp.bfloat16)
    context_low = (
        jnp.einsum("shqk,skhd->sqhd", probs_low, values, preferred_element_type=jnp.float32)
        .reshape(row_count, head_cols)
        .astype(jnp.bfloat16)
    )
    attn_part = jnp.einsum("tc,dc->td", context_low, out_low, preferred_element_type=jnp.float32)
    attn_sum = lax.psum(attn_part, "tensor")
    residual_one = tokens_in.astype(jnp.float32) + attn_sum + biases[2]
    normed = layer_norm(residual_one, gains[0], biases[3])
    normed_low = normed.astype(jnp.bfloat16)
    pre_act = jnp.dot(normed_low, in_low, preferred_element_type=jnp.float32) + bias_hidden
    act_low = exact_gelu(pre_act).astype(jnp.bfloat16)
    down_part = jnp.einsum("tf,df->td", act_low, down_low, preferred_element_type=jnp.float32)
    down_sum = lax.psum(down_part, "tensor")
    residual_two = normed + down_sum + biases[4]
    live = inside.astype(jnp.int32) * span_mask.reshape(seq_count, seq_length) > 0
    upto = (positions[:, None] <= positions[None, :]).astype(jnp.float32)
    rank = jnp.dot(live.astype(jnp.float32), upto).astype(jnp.int32) - 1
    slots = jnp.arange(SPAN_ROWS, dtype=jnp.int32)
    pick = (live[:, None, :] & (rank[:, None, :] == slots[None, :, None])).astype(jnp.float32)
    pick_low = pick.astype(jnp.bfloat16)

    def rows_of(values):
        width = values.shape[-1]
        return jnp.einsum(
            "srt,std->srd",
            pick,
            values.reshape(seq_count, seq_length, width),
            precision=lax.Precision.HIGHEST,
        ).reshape(seq_count * SPAN_ROWS, width)

    def low_rows_of(values):
        width = values.shape[-1]
        return jnp.einsum(
            "srt,std->srd",
            pick_low,
            values.reshape(seq_count, seq_length, width),
            preferred_element_type=jnp.bfloat16,
        ).reshape(seq_count * SPAN_ROWS, width)

    result = layer_norm(residual_two, gains[1], biases[5])
    normed_out = result.astype(jnp.bfloat16)
    residual_one_rows = rows_of(residual_one)
    residual_two_rows = rows_of(residual_two)
    grad_result = low_rows_of(cotangent).astype(jnp.float32)
    _, norm_two_back = jax.vjp(layer_norm, residual_two_rows, gains[1], biases[5])
    d_res_two, d_gain_two, d_shift_two = norm_two_back(grad_result)
    d_res_two_low = d_res_two.astype(jnp.bfloat16)
    normed_low_rows = low_rows_of(normed_low)
    pre_rows = jnp.dot(normed_low_rows, in_low, preferred_element_type=jnp.float32) + bias_hidden
    act_rows, gelu_back = jax.vjp(exact_gelu, pre_rows)
    grad_back = outer_sum(d_res_two_low, act_rows.astype(jnp.bfloat16))
    d_act = jnp.dot(d_res_two_low, down_low, preferred_element_type=jnp.float32)
    d_pre = gelu_back(d_act)[0]
    d_pre_low = d_pre.astype(jnp.bfloat16)
    grad_in = outer_sum(normed_low_rows, d_pre_low)
    d_normed_part = jnp.einsum("tf,df->td", d_pre_low, in_low, preferred_element_type=jnp.float32)
    d_normed = lax.psum(d_normed_part, "tensor") + d_res_two
    _, norm_one_back = jax.vjp(layer_norm, residual_one_rows, gains[0], biases[3])
    d_res_one, d_gain_one, d_shift_one = norm_one_back(d_normed)
    d_res_one_low = d_res_one.astype(jnp.bfloat16)
    grad_out_proj = outer_sum(d_res_one_low, low_rows_of(context_low))
    row_shape = (seq_count, SPAN_ROWS, local_heads, head_size)
    d_context = (
        jnp.dot(d_res_one_low, out_low, preferred_element_type=jnp.float32)
        .astype(jnp.bfloat16)
        .reshape(row_shape)
    )
    query_rows = low_rows_of(queries.reshape(row_count, head_cols)).reshape(row_shape)
    raw = jnp.einsum("sqhd,skhd->shqk", query_rows, keys, preferred_element_type=jnp.float32)
    probs = jax.nn.softmax(raw + key_bias[:, None, None, :], axis=-1)
    probs_again = probs.astype(jnp.bfloat16)
    d_probs = jnp.einsum("sqhd,skhd->shqk", d_context, values, preferred_element_type=jnp.float32)
    d_values = jnp.einsum(
        "shqk,sqhd->skhd", probs_again, d_context, preferred_element_type=jnp.float32
    ).reshape(row_count, head_cols)
    d_scores = (probs * (d_probs - jnp.sum(probs * d_probs, axis=-1, keepdims=True))).astype(
        jnp.bfloat16
    )
    d_queries = (
        jnp.einsum("shqk,skhd->sqhd", d_scores, keys, preferred_element_type=jnp.float32).reshape(
            seq_count * SPAN_ROWS, head_cols
        )
        * query_scale
    )
    d_keys = jnp.einsum(
        "shqk,sqhd->skhd", d_scores, query_rows, preferred_element_type=jnp.float32
    ).reshape(row_count, head_cols)

    def spread(row_values):
        width = row_values.shape[-1]
        return jnp.einsum(
            "srt,srd->std",
            pick,
            row_values.reshape(seq_count, SPAN_ROWS, width),
            precision=lax.Precision.HIGHEST,
        ).reshape(row_count, width)

    d_proj_low = (
        jnp.stack([spread(d_queries), d_keys, d_values], axis=1)
        .astype(jnp.bfloat16)
        .reshape(row_count, 3 * head_cols)
    )
    grad_qkv = outer_sum(tokens_in, d_proj_low).reshape(model_width, 3, head_cols)
    d_entry_part = jnp.einsum("tc,dc->td", d_proj_low, qkv_low, preferred_element_type=jnp.float32)
    input_grad = lax.psum(d_entry_part, "tensor") + spread(d_res_one)
    first_rank = (tensor_slot == 0).astype(jnp.float32)
    width_zero = jnp.zeros((model_width,), jnp.float32)

    def place_heads(partial_sum):
        return lax.dynamic_update_slice_in_dim(width_zero, partial_sum, tensor_slot * head_cols, 0)

    grad_gains = jnp.stack([d_gain_one, d_gain_two]) * first_rank
    grad_biases = jnp.stack(
        [
            place_heads(jnp.sum(d_queries, axis=0)),
            place_heads(jnp.sum(d_values, axis=0)),
            jnp.sum(d_res_one, axis=0) * first_rank,
            d_shift_one * first_rank,
            jnp.sum(d_res_two, axis=0) * first_rank,
            d_shift_two * first_rank,
        ]
    )
    grad_bias_in = lax.dynamic_update_slice_in_dim(
        jnp.zeros(bias_in.shape, jnp.float32), jnp.sum(d_pre, axis=0), tensor_slot * hidden_cols, 0
    )
    grad_gains, grad_biases, grad_bias_in = lax.psum(
        (grad_gains, grad_biases, grad_bias_in), ("dp", "tensor")
    )
    data_slot = lax.axis_index("dp")
    shard_rows = model_width // lax.axis_size("dp")
    owned = tuple(
        (
            lax.psum_scatter(part, "dp", scatter_dimension=0, tiled=True)
            for part in (grad_qkv, grad_out_proj, grad_in, grad_back)
        )
    )
    clock = step[0].astype(jnp.float32)
    warm = warmup[0].astype(jnp.float32)
    horizon = total[0].astype(jnp.float32)
    ratio = jnp.minimum(clock / warm, (horizon - clock) / (horizon - warm))
    corr_one = 1.0 - jnp.power(BETA_ONE, clock)
    corr_two = 1.0 - jnp.power(BETA_TWO, clock)
    change_rows = []
    fresh_moments = []
    for weight, grad_rows, moment in zip(
        (w_qkv, w_out, w_in, w_back), owned, (mom_qkv, mom_out, mom_in, mom_back)
    ):
        weight_rows = lax.dynamic_slice_in_dim(weight, data_slot * shard_rows, shard_rows, 0)
        row_change, new_moment = adam_step(
            weight_rows, grad_rows, moment, ratio, corr_one, corr_two, WEIGHT_DECAY
        )
        change_rows.append(row_change)
        fresh_moments.append(new_moment)
    change_qkv, change_out_proj, change_in_proj, change_back_proj = (
        lax.all_gather(change_rows[0], "dp", axis=0, tiled=True),
        lax.all_gather(change_rows[1], "dp", axis=0, tiled=True),
        lax.all_gather(change_rows[2], "dp", axis=0, tiled=True),
        lax.all_gather(change_rows[3], "dp", axis=0, tiled=True),
    )
    change_gains, new_mom_gains = adam_step(
        gains, grad_gains, mom_gains, ratio, corr_one, corr_two, 0.0
    )
    change_biases, new_mom_biases = adam_step(
        biases, grad_biases, mom_biases, ratio, corr_one, corr_two, 0.0
    )
    change_bias_in, new_mom_bias_in = adam_step(
        bias_in, grad_bias_in, mom_bias_in, ratio, corr_one, corr_two, 0.0
    )
    return (
        normed_out,
        input_grad,
        change_qkv,
        change_out_proj,
        change_in_proj,
        change_back_proj,
        change_gains,
        change_biases,
        change_bias_in,
        fresh_moments[0],
        fresh_moments[1],
        fresh_moments[2],
        fresh_moments[3],
        new_mom_gains,
        new_mom_biases,
        new_mom_bias_in,
    )


def solution(mesh):
    in_specs = (
        P("dp", None),
        P("dp", None),
        P("dp"),
        P("dp"),
        P(),
        P(),
        P(),
        P(None, None, "tensor"),
        P(None, "tensor"),
        P(None, "tensor"),
        P(None, "tensor"),
        P(),
        P(),
        P(),
        P(None, "dp", None, "tensor"),
        P(None, "dp", "tensor"),
        P(None, "dp", "tensor"),
        P(None, "dp", "tensor"),
        P(),
        P(),
        P(),
    )
    out_specs = (
        P("dp", None),
        P("dp", None),
        P(None, None, "tensor"),
        P(None, "tensor"),
        P(None, "tensor"),
        P(None, "tensor"),
        P(),
        P(),
        P(),
        P(None, "dp", None, "tensor"),
        P(None, "dp", "tensor"),
        P(None, "dp", "tensor"),
        P(None, "dp", "tensor"),
        P(),
        P(),
        P(),
    )
    return jax.shard_map(
        on_device, mesh=mesh, in_specs=in_specs, out_specs=out_specs, check_vma=False
    )
```

profile of v0, /device:TPU:0, one launch (start us, length us, event | category | flops | bytes accessed | tf_op | source)
XLA Modules:
  0.0 894.0 jit_solution(5073173420024962855)
XLA Ops:
  7.2 3.9 fusion.15
  13.9 2.1 convert_element_type.129
  16.0 1.7 squeeze.7
  18.3 1.8 fusion.168
  20.9 1.8 multiply_convert_fusion
  22.7 2.8 add_reduce_fusion
  25.6 1.8 exponential_reduce_fusion
  27.3 1.8 copy-done.3
  29.8 2.8 squeeze.6
  32.7 1.8 add_convert_fusion.1
  34.5 5.7 fusion.20
  41.2 3.0 fusion.96
  46.6 94.5 %all-reduce.6.cloned.1.call-done = f32[1536,768]{1,0:T(8,128)} async-done(((f32[1536,768]{1,0:T(8,128)}), f32[1536,768]{1,0:T(8,128)}) %all-reduce.6.cloned.1.call-update) | async-done | bytes 4718608 | tf_op jit(solution)/shard_map/psum | solution.py:103
  141.1 3.8 fusion.167
  145.7 1.4 copy-done.2
  147.1 2.1 fusion.14
  149.2 17.8 %fusion.18 = f32[1536,768]{1,0:T(8,128)} fusion(bf16[1536,768]{1,0:T(8,128)(2,1)} %fusion.14, f32[768]{0:T(1024)} %dynamic_slice.23, f32[768,768]{1,0:T(8,128)} %param.31, f32[768,768]{1,0:T(8,128)} %param.30), kind=kOutput, calls=%fused_computation.39 | convolution fusion | flops 3702915072 | bytes 11799552 | tf_op jit(solution)/shard_map/tf,df->td/dot_general | solution.py:109
  167.2 1.8 squeeze.8
  170.6 2.0 fusion.35
  172.6 3.1 fusion.175
  175.7 4.6 fusion.173
  183.3 78.0 %all-reduce.8.cloned.1.call-done = f32[1536,768]{1,0:T(8,128)} async-done(((f32[1536,768]{1,0:T(8,128)}), f32[1536,768]{1,0:T(8,128)}) %all-reduce.8.cloned.1.call-update) | async-done | bytes 4718608 | tf_op jit(solution)/shard_map/psum | solution.py:110
  261.3 5.3 fusion.166
  266.7 2.2 copy-done.4
  268.9 2.1 fusion.174
  271.0 2.0 multiply_reduce_fusion.8
  273.2 1.4 fusion.100
  274.8 1.4 fusion.25
  276.3 4.8 fusion.180
  283.3 33.8 %all-reduce.10.cloned.1.call-done = f32[240,768]{1,0:T(8,128)} async-done(((f32[240,768]{1,0:T(8,128)}), f32[240,768]{1,0:T(8,128)}) %all-reduce.10.cloned.1.call-update) | async-done | bytes 737296 | tf_op jit(solution)/shard_map/psum | solution.py:154
  317.0 2.2 fusion.163
  320.9 1.5 convolution_convert_fusion.1
  323.2 2.6 fusion.179
  327.9 1.7 fusion.178
  330.9 1.8 copy.94
  332.7 1.5 stack_reshape.10
  334.2 1.6 fusion.49
  336.3 1.5 stack_reshape.9
  337.9 1.4 maximum_convert_fusion
  339.3 4.4 fusion.181
  343.7 3.0 copy.97
  346.8 1.9 fusion.89
  348.8 4.6 fusion.62
  355.3 6.1 convolution_bitcast_fusion
  365.0 51.3 %reduce-scatter.5.cloned.1.call-done = f32[96,3,192]{2,0,1:T(8,128)} async-done(((f32[768,3,192]{2,0,1:T(8,128)}), f32[96,3,192]{2,0,1:T(8,128)}) %reduce-scatter.5.cloned.1.call-update) | async-done | bytes 221200 | tf_op jit(solution)/shard_map/reduce_scatter | solution.py:230
  416.3 2.2 fusion.104
  418.5 69.8 %reduce-scatter.9.cloned.1.call-done = f32[96,768]{1,0:T(8,128)} async-done(((f32[768,768]{1,0:T(8,128)}), f32[96,768]{1,0:T(8,128)}) %reduce-scatter.9.cloned.1.call-update) | async-done | bytes 294928 | tf_op jit(solution)/shard_map/reduce_scatter | solution.py:230
  488.3 2.2 fusion.105
  492.8 3.0 multiply_reduce_fusion
  495.9 4.2 add_convert_fusion
  500.1 59.7 %reduce-scatter.11.cloned.1.call-done = f32[96,768]{1,0:T(8,128)} async-done(((f32[768,768]{1,0:T(8,128)}), f32[96,768]{1,0:T(8,128)}) %reduce-scatter.11.cloned.1.call-update) | async-done | bytes 294928 | tf_op jit(solution)/shard_map/reduce_scatter | solution.py:230
  559.9 2.0 fusion.106
  562.9 40.3 %all-reduce = (f32[2,768]{1,0:T(2,128)S(1)}, f32[6,768]{1,0:T(8,128)S(1)}, f32[3072]{0:T(1024)S(1)}) all-reduce(f32[2,768]{1,0:T(2,128)S(1)} %maximum_multiply_fusion, f32[6,768]{1,0:T(8,128)S(1)} %stack.88, f32[3072]{0:T(1024)S(1)} %dynamic_update_slice.13), channel_id=1, replica_groups=mesh['dp'=8,'tensor'=4] {'dp','tensor'}, use_global_device_ids=true, to_apply=%region_27.28 | all-reduce | flops 9216 | bytes 73728 | tf_op jit(solution)/shard_map/psum | solution.py:223
  607.0 4.3 fusion.47
  611.3 13.9 %reduce-scatter.7.cloned.1.call-done = f32[96,192]{1,0:T(8,128)} async-done(((f32[768,192]{1,0:T(8,128)}), f32[96,192]{1,0:T(8,128)}) %reduce-scatter.7.cloned.1.call-update) | async-done | bytes 73744 | tf_op jit(solution)/shard_map/reduce_scatter | solution.py:230
  626.3 32.2 %all_gather.13 = f32[768,192]{1,0:T(8,128)S(1)} all-gather(f32[96,192]{1,0:T(8,128)S(1)} %get-tuple-element.107), channel_id=1, replica_groups=mesh['dp'=8,'tensor'=4] {'dp'}, dimensions={0}, use_global_device_ids=true | all-gather | bytes 663552 | tf_op jit(solution)/shard_map/all_gather | solution.py:253
  660.3 60.5 %all-reduce.12.cloned.1.call-done = f32[1536,768]{1,0:T(8,128)} async-done(((f32[1536,768]{1,0:T(8,128)}), f32[1536,768]{1,0:T(8,128)}) %all-reduce.12.cloned.1.call-update) | async-done | bytes 4718608 | tf_op jit(solution)/shard_map/psum | solution.py:202
  720.8 6.6 bitcast_add_fusion
  729.9 46.0 %all-gather.4.cloned.1.call-done = f32[768,3,192]{2,0,1:T(8,128)} async-done(((f32[96,3,192]{2,0,1:T(8,128)}), f32[768,3,192]{2,0,1:T(8,128)}) %all-gather.4.cloned.1.call-update) | async-done | bytes 1769488 | tf_op jit(solution)/shard_map/all_gather | solution.py:252
  775.9 2.9 copy.102
  778.8 50.6 %all-gather.6.cloned.1.call-done = f32[768,768]{1,0:T(8,128)} async-done(((f32[96,768]{1,0:T(8,128)}), f32[768,768]{1,0:T(8,128)}) %all-gather.6.cloned.1.call-update) | async-done | bytes 2359312 | tf_op jit(solution)/shard_map/all_gather | solution.py:254
  829.4 53.1 %all-gather.8.cloned.1.call-done = f32[768,768]{1,0:T(8,128)} async-done(((f32[96,768]{1,0:T(8,128)}), f32[768,768]{1,0:T(8,128)}) %all-gather.8.cloned.1.call-update) | async-done | bytes 2359312 | tf_op jit(solution)/shard_map/all_gather | solution.py:255
  882.5 3.4 copy.181
  885.9 1.4 copy.182
  (237 shorter events, 38.6 us)
Async XLA Ops:
  7.2 263.8 %copy-start = (bf16[1536,768]{1,0:T(8,128)(2,1)S(1)}, bf16[1536,768]{1,0:T(8,128)(2,1)}, u32[]{:S(2)}) copy-start(bf16[1536,768]{1,0:T(8,128)(2,1)} %param.22) | copy-start | bytes 7077892
  7.2 133.9 %all-reduce.6.cloned.1.call-start = ((), (), s32[]{:S(2)}) async-start(), calls=%async_computation.4 | async-start | bytes 9437184 | tf_op jit(solution)/shard_map/psum | solution.py:103
  11.2 2.7 copy-start.63
  25.5 3.6 copy-start.3
  25.5 7.0 copy-start.60
  34.4 5.7 copy-start.15
  34.4 6.7 copy-start.19
  44.2 217.1 %all-reduce.8.cloned.1.call-start = ((), (), s32[]{:S(2)}) async-start(), calls=%async_computation.5 | async-start | bytes 9437184 | tf_op jit(solution)/shard_map/psum | solution.py:110
  144.9 2.2 copy-start.2
  167.0 150.0 %all-reduce.10.cloned.1.call-start = ((), (), s32[]{:S(2)}) async-start(), calls=%async_computation.6 | async-start | bytes 1474560 | tf_op jit(solution)/shard_map/psum | solution.py:154
  172.6 9.3 %copy-start.26 = (bf16[3,80,192]{1,2,0:T(8,128)(2,1)}, bf16[3,80,192]{1,2,0:T(8,128)(2,1)S(1)}, u32[]{:S(2)}) copy-start(bf16[3,80,192]{1,2,0:T(8,128)(2,1)S(1)} %fusion.35) | copy-start | bytes 276484
  175.7 5.7 copy-start.10
  175.7 6.2 copy-start.8
  175.7 6.2 copy-start.55
  180.3 81.0 %copy-start.31 = (f32[1536]{0:T(1024)S(1)}, f32[1536]{0:T(1024)}, u32[]{:S(2)}) copy-start(f32[1536]{0:T(1024)} %copy-done.30) | copy-start | bytes 18436
  180.3 81.0 %copy-start.35 = (f32[1536]{0:T(1024)S(1)}, f32[1536]{0:T(1024)}, u32[]{:S(2)}) copy-start(f32[1536]{0:T(1024)} %copy-done.34) | copy-start | bytes 18436
  180.3 81.0 %copy-start.40 = (f32[768]{0:T(1024)S(1)}, f32[768]{0:T(1024)}, u32[]{:S(2)}) copy-start(f32[768]{0:T(1024)} %get-tuple-element.118) | copy-start | bytes 9220
  180.3 81.0 %copy-start.57 = (f32[768]{0:T(1024)S(1)}, f32[768]{0:T(1024)}, u32[]{:S(2)}) copy-start(f32[768]{0:T(1024)} %get-tuple-element.119) | copy-start | bytes 9220
  266.7 2.2 copy-start.4
  273.2 7.9 copy-start.45
  273.2 7.9 copy-start.47
  274.6 6.4 copy-start.49
  276.3 4.8 copy-start.17
  276.3 4.8 copy-start.9
  281.0 2.2 copy-start.23
  282.5 133.8 %reduce-scatter.5.cloned.1.call-start = ((), (), s32[]{:S(2)}) async-start(), calls=%async_computation.8 | async-start | bytes 2654208 | tf_op jit(solution)/shard_map/reduce_scatter | solution.py:230
  320.9 4.9 copy-start.11
  323.2 2.6 copy-start.16
  323.2 2.6 copy-start.29
  330.9 8.4 copy-start.21
  343.7 3.1 copy-start.24
  346.7 141.6 %reduce-scatter.9.cloned.1.call-start = ((), (), s32[]{:S(2)}) async-start(), calls=%async_computation.11 | async-start | bytes 2654208 | tf_op jit(solution)/shard_map/reduce_scatter | solution.py:230
  348.8 4.7 copy-start.14
  348.8 211.1 %reduce-scatter.11.cloned.1.call-start = ((), (), s32[]{:S(2)}) async-start(), calls=%async_computation.13 | async-start | bytes 2654208 | tf_op jit(solution)/shard_map/reduce_scatter | solution.py:230
  353.4 271.8 %reduce-scatter.7.cloned.1.call-start = ((), (), s32[]{:S(2)}) async-start(), calls=%async_computation.10 | async-start | bytes 884736 | tf_op jit(solution)/shard_map/reduce_scatter | solution.py:230
  355.0 365.8 %all-reduce.12.cloned.1.call-start = ((), (), s32[]{:S(2)}) async-start(), calls=%async_computation.7 | async-start | bytes 9437184 | tf_op jit(solution)/shard_map/psum | solution.py:202
  361.3 130.4 %copy-start.38 = (f32[2,6,768]{2,0,1:T(2,128)S(1)}, f32[2,6,768]{2,0,1:T(2,128)}, u32[]{:S(2)}) copy-start(f32[2,6,768]{2,0,1:T(2,128)} %param.40) | copy-start | bytes 110596
  361.3 130.4 %copy-start.42 = (f32[2,3072]{1,0:T(2,128)S(1)}, f32[2,3072]{1,0:T(2,128)}, u32[]{:S(2)}) copy-start(f32[2,3072]{1,0:T(2,128)} %param.41) | copy-start | bytes 73732
  361.3 131.0 %copy-start.7 = (f32[3,80,768]{2,1,0:T(8,128)S(1)}, f32[3,80,768]{2,1,0:T(8,128)}, u32[]{:S(2)}) copy-start(f32[3,80,768]{2,1,0:T(8,128)} %get-tuple-element.137) | copy-start | bytes 2211844
  361.3 131.0 %copy-start.46 = (f32[3,80]{1,0:T(4,128)S(1)}, f32[3,80]{1,0:T(4,128)}, u32[]{:S(2)}) copy-start(f32[3,80]{1,0:T(4,128)} %copy-done.45) | copy-start | bytes 2884
  361.3 131.0 %copy-start.48 = (f32[3,80]{1,0:T(4,128)S(1)}, f32[3,80]{1,0:T(4,128)}, u32[]{:S(2)}) copy-start(f32[3,80]{1,0:T(4,128)} %copy-done.47) | copy-start | bytes 2884
  361.3 131.0 %copy-start.50 = (f32[3,80]{1,0:T(4,128)S(1)}, f32[3,80]{1,0:T(4,128)}, u32[]{:S(2)}) copy-start(f32[3,80]{1,0:T(4,128)} %copy-done.49) | copy-start | bytes 2884
  361.4 131.4 %copy-start.41 = (f32[1536]{0:T(1024)S(1)}, f32[1536]{0:T(1024)}, u32[]{:S(2)}) copy-start(f32[1536]{0:T(1024)} %get-tuple-element.88) | copy-start | bytes 18436
  361.4 414.5 %all-gather.4.cloned.1.call-start = ((), (), s32[]{:S(2)}) async-start(), calls=%async_computation.9 | async-start | bytes 2654208 | tf_op jit(solution)/shard_map/all_gather | solution.py:252
  418.4 77.3 %copy-start.51 = (f32[768]{0:T(1024)S(1)}, f32[768]{0:T(1024)}, u32[]{:S(2)}) copy-start(f32[768]{0:T(1024)} %get-tuple-element.120) | copy-start | bytes 9220
  418.5 410.9 %all-gather.6.cloned.1.call-start = ((), (), s32[]{:S(2)}) async-start(), calls=%async_computation.12 | async-start | bytes 2654208 | tf_op jit(solution)/shard_map/all_gather | solution.py:254
  490.5 392.0 %all-gather.8.cloned.1.call-start = ((), (), s32[]{:S(2)}) async-start(), calls=%async_computation.14 | async-start | bytes 2654208 | tf_op jit(solution)/shard_map/all_gather | solution.py:255
  495.7 64.1 %copy-start.28 = (f32[2,96,768]{2,1,0:T(8,128)S(1)}, f32[2,96,768]{2,1,0:T(8,128)}, u32[]{:S(2)}) copy-start(f32[2,96,768]{2,1,0:T(8,128)} %param.38) | copy-start | bytes 1769476
  495.8 66.1 %copy-start.56 = (f32[768]{0:T(1024)S(1)}, f32[768]{0:T(1024)}, u32[]{:S(2)}) copy-start(f32[768]{0:T(1024)} %get-tuple-element.70) | copy-start | bytes 9220
  495.8 66.2 %copy-start.59 = (f32[768]{0:T(1024)S(1)}, f32[768]{0:T(1024)}, u32[]{:S(2)}) copy-start(f32[768]{0:T(1024)} %get-tuple-element.146) | copy-start | bytes 9220
  495.8 66.5 %copy-start.52 = (f32[768]{0:T(1024)S(1)}, f32[768]{0:T(1024)}, u32[]{:S(2)}) copy-start(f32[768]{0:T(1024)} %get-tuple-element.66) | copy-start | bytes 9220
  495.8 66.5 %copy-start.62 = (f32[3,64]{1,0:T(4,128)S(1)}, f32[3,64]{1,0:T(4,128)}, u32[]{:S(2)}) copy-start(f32[3,64]{1,0:T(4,128)} %get-tuple-element.142) | copy-start | bytes 2308
  495.8 66.5 %copy-start.61 = (f32[3,64]{1,0:T(4,128)S(1)}, f32[3,64]{1,0:T(4,128)}, u32[]{:S(2)}) copy-start(f32[3,64]{1,0:T(4,128)} %get-tuple-element.144) | copy-start | bytes 2308
  495.8 66.6 %copy-start.54 = (f32[768]{0:T(1024)S(1)}, f32[768]{0:T(1024)}, u32[]{:S(2)}) copy-start(f32[768]{0:T(1024)} %get-tuple-element.85) | copy-start | bytes 9220
  495.8 66.6 %copy-start.53 = (f32[768]{0:T(1024)S(1)}, f32[768]{0:T(1024)}, u32[]{:S(2)}) copy-start(f32[768]{0:T(1024)} %get-tuple-element.71) | copy-start | bytes 9220
  495.9 107.4 %copy-start.33 = (f32[6,768]{1,0:T(8,128)S(1)}, f32[6,768]{1,0:T(8,128)}, u32[]{:S(2)}) copy-start(f32[6,768]{1,0:T(8,128)} %param.33) | copy-start | bytes 55300
  495.9 108.7 %copy-start.43 = (f32[2,768]{1,0:T(2,128)S(1)}, f32[2,768]{1,0:T(2,128)}, u32[]{:S(2)}) copy-start(f32[2,768]{1,0:T(2,128)} %param.32) | copy-start | bytes 18436
  495.9 108.7 %copy-start.58 = (f32[2,2,768]{2,1,0:T(2,128)S(1)}, f32[2,2,768]{2,1,0:T(2,128)}, u32[]{:S(2)}) copy-start(f32[2,2,768]{2,1,0:T(2,128)} %param.39) | copy-start | bytes 36868
  495.9 109.9 %copy-start.36 = (f32[1,3072]{1,0:T(1,128)S(1)}, f32[1,3072]{1,0:T(1,128)}, u32[]{:S(2)}) copy-start(f32[1,3072]{1,0:T(1,128)} %get-tuple-element.113) | copy-start | bytes 36868
  495.9 109.9 %copy-start.37 = (f32[1,3072]{1,0:T(1,128)S(1)}, f32[1,3072]{1,0:T(1,128)}, u32[]{:S(2)}) copy-start(f32[1,3072]{1,0:T(1,128)} %get-tuple-element.114) | copy-start | bytes 36868
  495.9 109.9 %copy-start.44 = (f32[3072]{0:T(1024)S(1)}, f32[3072]{0:T(1024)}, u32[]{:S(2)}) copy-start(f32[3072]{0:T(1024)} %param.34) | copy-start | bytes 36868
  660.3 67.1 %copy-start.25 = (f32[1,96,3,192]{3,1,2,0:T(8,128)S(1)}, f32[1,96,3,192]{3,1,2,0:T(8,128)}, u32[]{:S(2)}) copy-start(f32[1,96,3,192]{3,1,2,0:T(8,128)} %get-tuple-element.103) | copy-start | bytes 663556
  882.5 3.4 copy-start.20
  882.5 4.8 copy-start.1
  (11 other events, 18.4 us)
Sparse Core Ops, SparseCore 0:
  44.3 96.7 all-reduce.5
  167.1 94.1 all-reduce.7
  282.6 34.3 all-reduce.9
  346.9 69.3 reduce-scatter.4
  420.2 68.0 reduce-scatter.8
  491.6 68.1 reduce-scatter.10
  563.7 61.4 reduce-scatter.6
  627.8 92.9 all-reduce.11
  723.8 52.0 all-gather.3
  778.8 50.5 all-gather.5
  831.8 50.5 all-gather.7
where the time goes:
time: 903 us; the launch traced here: 894 us
  waiting for transfers between devices  611 us (68%)
  matrix products  86.9 us (10%)
  blocking collectives  72.5 us (8%)
  other arithmetic  56.1 us (6%)
  local copies, waits for them, and re-layouts  48.5 us (5%)
  between operations  17.2 us (2%)
    reduce_scatter x4, waiting for transfers between devices, on_device(): lax.psum_scatter(part, 'dp', scatter_dimension=0, tiled=True)  195 us
    psum x1, waiting for transfers between devices, on_device(): attn_sum = lax.psum(attn_part, 'tensor')  94.5 us
    psum x1, waiting for transfers between devices, on_device(): down_sum = lax.psum(down_part, 'tensor')  78 us
    psum x1, waiting for transfers between devices, on_device(): input_grad = lax.psum(d_entry_part, 'tensor') + spread(d_res_one)  60.5 us
    all_gather x1, waiting for transfers between devices, on_device(): lax.all_gather(change_rows[3], 'dp', axis=0, tiled=True)  53.1 us
    all_gather x1, waiting for transfers between devices, on_device(): lax.all_gather(change_rows[2], 'dp', axis=0, tiled=True)  50.6 us
    all_gather x1, waiting for transfers between devices, on_device(): lax.all_gather(change_rows[0], 'dp', axis=0, tiled=True)  46 us
    psum x1, blocking collectives, on_device(): lax.psum((grad_gains, grad_biases, grad_bias_in), ('dp', 'tensor'))  40.3 us
  transfers between devices with their start and end apart: 11, of which 11 were waited for; matrix products, arithmetic and copies ran while one was open for 8% of the time, Pallas kernels for 0%

commit v1 on v0

--- a/solution.py
+++ b/solution.py
@@ -1,8 +1,10 @@
+import functools
 import math
 import jax
 import jax.numpy as jnp
 from jax import lax
 from jax.sharding import PartitionSpec as P
+from jax.lax import all_gather
 
 HD = 64
 SPAN_ROWS = 80
@@ -11,6 +13,14 @@
 BETA_TWO = 0.999
 ADAM_EPS = 1e-06
 WEIGHT_DECAY = 0.01
+
+
+def _carry_bench(q_in, named_axis):
+    frame_out = all_gather(q_in, named_axis).sum(axis=0)
+    return frame_out
+
+
+search_the_things = functools.partial(_carry_bench, named_axis="tensor")
 
 
 def layer_norm(values, gain, shift):
@@ -100,7 +110,7 @@
         .astype(jnp.bfloat16)
     )
     attn_part = jnp.einsum("tc,dc->td", context_low, out_low, preferred_element_type=jnp.float32)
-    attn_sum = lax.psum(attn_part, "tensor")
+    attn_sum = search_the_things(attn_part)
     residual_one = tokens_in.astype(jnp.float32) + attn_sum + biases[2]
     normed = layer_norm(residual_one, gains[0], biases[3])
     normed_low = normed.astype(jnp.bfloat16)

time: 903 us -> 950 us (1.052)
  other arithmetic: 56.1 us -> 81.4 us
  local copies, waits for them, and re-layouts: 48.5 us -> 70.9 us
    all_gather x0 -> x1, waiting for transfers between devices: none -> 120 us  [_carry_bench(): frame_out = all_gather(q_in, named_axis).sum(axis=0)]
    psum x1 -> x0, waiting for transfers between devices: 94.5 us -> none  [on_device(): attn_sum = lax.psum(attn_part, 'tensor')]
    reduce_scatter x4, waiting for transfers between devices: 195 us -> 170 us  [on_device(): lax.psum_scatter(part, 'dp', scatter_dimension=0, tiled=True)]
    reduce_sum x0 -> x1, other arithmetic: none -> 10.4 us  [_carry_bench(): frame_out = all_gather(q_in, named_axis).sum(axis=0)]
    unnamed x136 -> x116, local copies, waits for them, and re-layouts: 16.7 us -> 19.8 us
  transfers between devices with their start and end apart: 11 -> 11, of which waited for: 11 -> 10; matrix products, arithmetic and copies ran while one was open for 8% -> 11% of each run, Pallas kernels for 0% -> 0%
where the time goes in v1:
time: 950 us; the launch traced here: 941 us
  waiting for transfers between devices  607 us (64%)
  matrix products  90.2 us (9%)
  other arithmetic  81.4 us (9%)
  blocking collectives  73.2 us (8%)
  local copies, waits for them, and re-layouts  70.9 us (7%)
  between operations  16.8 us (2%)
    reduce_scatter x4, waiting for transfers between devices, on_device(): lax.psum_scatter(part, 'dp', scatter_dimension=0, tiled=True)  170 us
    all_gather x1, waiting for transfers between devices, _carry_bench(): frame_out = all_gather(q_in, named_axis).sum(axis=0)  120 us
    psum x1, waiting for transfers between devices, on_device(): down_sum = lax.psum(down_part, 'tensor')  78.4 us
    psum x1, waiting for transfers between devices, on_device(): input_grad = lax.psum(d_entry_part, 'tensor') + spread(d_res_one)  57.9 us
    all_gather x1, waiting for transfers between devices, on_device(): lax.all_gather(change_rows[3], 'dp', axis=0, tiled=True)  53.1 us
    all_gather x1, waiting for transfers between devices, on_device(): lax.all_gather(change_rows[2], 'dp', axis=0, tiled=True)  50 us
    all_gather x1, waiting for transfers between devices, on_device(): lax.all_gather(change_rows[0], 'dp', axis=0, tiled=True)  45.9 us
    psum x1, blocking collectives, on_device(): lax.psum((grad_gains, grad_biases, grad_bias_in), ('dp', 'tensor'))  41 us
  transfers between devices with their start and end apart: 11, of which 10 were waited for; matrix products, arithmetic and copies ran while one was open for 11% of the time, Pallas kernels for 0%

profile of v1, /device:TPU:0, one launch (start us, length us, event | category | flops | bytes accessed | tf_op | source)
XLA Modules:
  0.0 940.8 jit_solution(17461849073562420085)
XLA Ops:
  7.2 3.9 fusion.15
  14.5 2.1 convert_element_type.129
  16.6 1.7 squeeze.7
  18.9 2.5 fusion.168
  22.1 1.8 multiply_convert_fusion
  24.0 2.8 add_reduce_fusion
  26.8 1.8 exponential_reduce_fusion
  28.5 1.9 copy-done.2
  31.0 2.8 squeeze.6
  34.6 1.8 add_convert_fusion.1
  36.4 5.7 fusion.20
  43.1 3.0 fusion.96
  49.1 119.9 %all-gather.12.cloned.1.call-done = f32[6144,768]{1,0:T(8,128)} async-done(((f32[1536,768]{1,0:T(8,128)}), f32[6144,768]{1,0:T(8,128)}) %all-gather.12.cloned.1.call-update) | async-done | bytes 18874384 | tf_op jit(solution)/shard_map/all_gather | solution.py:19
  169.0 10.4 %reduce_sum.224 = f32[1536,768]{1,0:T(8,128)} reduce(f32[4,1536,768]{2,1,0:T(8,128)} %bitcast.206, f32[]{:T(128)} %constant.60.clone.1), dimensions={0}, to_apply=%region_2.3 | reduce | flops 3538944 | bytes 23592964 | tf_op jit(solution)/shard_map/reduce_sum | solution.py:19
  179.4 3.8 fusion.167
  185.4 2.1 fusion.14
  187.5 17.8 %fusion.18 = f32[1536,768]{1,0:T(8,128)} fusion(bf16[1536,768]{1,0:T(8,128)(2,1)} %fusion.14, f32[768]{0:T(1024)} %dynamic_slice.23, f32[768,768]{1,0:T(8,128)} %param.31, f32[768,768]{1,0:T(8,128)} %param.30), kind=kOutput, calls=%fused_computation.39 | convolution fusion | flops 3702915072 | bytes 11799552 | tf_op jit(solution)/shard_map/tf,df->td/dot_general | solution.py:119
  205.6 1.8 squeeze.8
  208.2 2.0 fusion.35
  210.2 3.2 fusion.175
  213.4 4.6 fusion.173
  221.0 78.4 %all-reduce.5.cloned.1.call-done = f32[1536,768]{1,0:T(8,128)} async-done(((f32[1536,768]{1,0:T(8,128)}), f32[1536,768]{1,0:T(8,128)}) %all-reduce.5.cloned.1.call-update) | async-done | bytes 4718608 | tf_op jit(solution)/shard_map/psum | solution.py:120
  299.5 5.3 fusion.166
  304.8 2.2 copy-done.3
  307.0 2.1 fusion.174
  309.2 2.0 multiply_reduce_fusion.8
  314.5 4.8 fusion.180
  322.0 2.1 bitcast_subtract_fusion
  324.1 31.8 %all-reduce.7.cloned.1.call-done = f32[240,768]{1,0:T(8,128)} async-done(((f32[240,768]{1,0:T(8,128)}), f32[240,768]{1,0:T(8,128)}) %all-reduce.7.cloned.1.call-update) | async-done | bytes 737296 | tf_op jit(solution)/shard_map/psum | solution.py:164
  355.9 2.5 fusion.163
  358.4 2.1 multiply_reduce_fusion.4
  363.2 1.7 reshape.459
  364.9 2.7 fusion.179
  369.6 1.7 fusion.178
  372.6 2.5 stack_reshape.11
  375.2 2.5 copy.94
  377.6 2.5 stack_reshape.10
  383.1 2.5 stack_reshape.9
  387.2 4.4 fusion.181
  391.7 2.9 copy.97
  394.7 2.9 fusion.89
  397.7 4.7 fusion.62
  403.9 2.3 fusion.86
  406.4 6.3 convolution_bitcast_fusion
  417.0 47.0 %reduce-scatter.5.cloned.1.call-done = f32[96,3,192]{2,0,1:T(8,128)} async-done(((f32[768,3,192]{2,0,1:T(8,128)}), f32[96,3,192]{2,0,1:T(8,128)}) %reduce-scatter.5.cloned.1.call-update) | async-done | bytes 221200 | tf_op jit(solution)/shard_map/reduce_scatter | solution.py:240
  464.0 2.2 fusion.104
  466.3 69.6 %reduce-scatter.9.cloned.1.call-done = f32[96,768]{1,0:T(8,128)} async-done(((f32[768,768]{1,0:T(8,128)}), f32[96,768]{1,0:T(8,128)}) %reduce-scatter.9.cloned.1.call-update) | async-done | bytes 294928 | tf_op jit(solution)/shard_map/reduce_scatter | solution.py:240
  535.9 2.2 fusion.105
  543.8 2.1 add_reduce_fusion.1
  547.2 3.0 multiply_reduce_fusion
  550.2 4.0 add_convert_fusion
  554.2 53.1 %reduce-scatter.11.cloned.1.call-done = f32[96,768]{1,0:T(8,128)} async-done(((f32[768,768]{1,0:T(8,128)}), f32[96,768]{1,0:T(8,128)}) %reduce-scatter.11.cloned.1.call-update) | async-done | bytes 294928 | tf_op jit(solution)/shard_map/reduce_scatter | solution.py:240
  607.3 2.3 fusion.106
  622.3 41.0 %all-reduce = (f32[2,768]{1,0:T(2,128)}, f32[6,768]{1,0:T(8,128)}, f32[3072]{0:T(1024)}) all-reduce(f32[2,768]{1,0:T(2,128)} %maximum_multiply_fusion, f32[6,768]{1,0:T(8,128)S(1)} %stack.88, f32[3072]{0:T(1024)} %copy-done.42), channel_id=1, replica_groups=mesh['dp'=8,'tensor'=4] {'dp','tensor'}, use_global_device_ids=true, to_apply=%region_27.28 | all-reduce | flops 9216 | bytes 73728 | tf_op jit(solution)/shard_map/psum | solution.py:233
  669.3 4.3 fusion.47
  673.6 1.7 fusion.110
  675.3 32.3 %all_gather.21 = f32[768,192]{1,0:T(8,128)S(1)} all-gather(f32[96,192]{1,0:T(8,128)S(1)} %get-tuple-element.107), channel_id=1, replica_groups=mesh['dp'=8,'tensor'=4] {'dp'}, dimensions={0}, use_global_device_ids=true | all-gather | bytes 663552 | tf_op jit(solution)/shard_map/all_gather | solution.py:263
  710.3 57.9 %all-reduce.9.cloned.1.call-done = f32[1536,768]{1,0:T(8,128)} async-done(((f32[1536,768]{1,0:T(8,128)}), f32[1536,768]{1,0:T(8,128)}) %all-reduce.9.cloned.1.call-update) | async-done | bytes 4718608 | tf_op jit(solution)/shard_map/psum | solution.py:212
  768.2 6.6 bitcast_add_fusion
  777.4 45.9 %all-gather.6.cloned.1.call-done = f32[768,3,192]{2,0,1:T(8,128)} async-done(((f32[96,3,192]{2,0,1:T(8,128)}), f32[768,3,192]{2,0,1:T(8,128)}) %all-gather.6.cloned.1.call-update) | async-done | bytes 1769488 | tf_op jit(solution)/shard_map/all_gather | solution.py:262
  823.4 2.9 copy.102
  826.3 50.0 %all-gather.8.cloned.1.call-done = f32[768,768]{1,0:T(8,128)} async-done(((f32[96,768]{1,0:T(8,128)}), f32[768,768]{1,0:T(8,128)}) %all-gather.8.cloned.1.call-update) | async-done | bytes 2359312 | tf_op jit(solution)/shard_map/all_gather | solution.py:264
  876.3 53.1 %all-gather.10.cloned.1.call-done = f32[768,768]{1,0:T(8,128)} async-done(((f32[96,768]{1,0:T(8,128)}), f32[768,768]{1,0:T(8,128)}) %all-gather.10.cloned.1.call-update) | async-done | bytes 2359312 | tf_op jit(solution)/shard_map/all_gather | solution.py:265
  929.3 3.4 copy.181
  (218 shorter events, 69.4 us)
Async XLA Ops:
  7.2 302.0 %copy-start = (bf16[1536,768]{1,0:T(8,128)(2,1)S(1)}, bf16[1536,768]{1,0:T(8,128)(2,1)}, u32[]{:S(2)}) copy-start(bf16[1536,768]{1,0:T(8,128)(2,1)} %param.22) | copy-start | bytes 7077892
  7.2 161.8 %all-gather.12.cloned.1.call-start = ((), (), s32[]{:S(2)}) async-start(), calls=%async_computation.14 | async-start | bytes 23592960 | tf_op jit(solution)/shard_map/all_gather | solution.py:19
  11.2 2.1 copy-start.36
  11.2 3.3 copy-start.53
  14.4 169.6 %copy-start.43 = (f32[768]{0:T(1024)}, f32[768]{0:T(1024)S(1)}, u32[]{:S(2)}) copy-start(f32[768]{0:T(1024)S(1)} %get-tuple-element.118) | copy-start | bytes 9220
  26.8 3.6 copy-start.2
  36.4 5.7 copy-start.14
  36.4 6.7 copy-start.17
  42.1 0.8 copy-start.13
  46.2 253.3 %all-reduce.5.cloned.1.call-start = ((), (), s32[]{:S(2)}) async-start(), calls=%async_computation.4 | async-start | bytes 9437184 | tf_op jit(solution)/shard_map/psum | solution.py:120
  49.1 134.9 %copy-start.30 = (f32[768]{0:T(1024)}, f32[768]{0:T(1024)S(1)}, u32[]{:S(2)}) copy-start(f32[768]{0:T(1024)S(1)} %get-tuple-element.78) | copy-start | bytes 9220
  183.2 2.2 copy-start.1
  183.3 2.2 copy-start.32
  184.0 1.4 copy-start.38
  205.3 2.1 copy-start.52
  205.3 150.6 %all-reduce.7.cloned.1.call-start = ((), (), s32[]{:S(2)}) async-start(), calls=%async_computation.5 | async-start | bytes 1474560 | tf_op jit(solution)/shard_map/psum | solution.py:164
  208.1 194.4 %copy-start.34 = (pred[3,512]{1,0:T(4,128)(4,1)}, pred[3,512]{1,0:T(4,128)(4,1)S(1)}, u32[]{:S(2)}) copy-start(pred[3,512]{1,0:T(4,128)(4,1)S(1)} %select_compare_fusion) | copy-start | bytes 4612
  210.2 9.4 copy-start.26
  213.4 5.7 copy-start.10
  213.4 6.2 copy-start.8
  213.4 6.2 copy-start.50
  218.0 0.9 copy-start.6
  218.0 81.5 %copy-start.31 = (f32[768]{0:T(1024)S(1)}, f32[768]{0:T(1024)}, u32[]{:S(2)}) copy-start(f32[768]{0:T(1024)} %copy-done.30) | copy-start | bytes 9220
  218.0 81.5 %copy-start.33 = (f32[1536]{0:T(1024)S(1)}, f32[1536]{0:T(1024)}, u32[]{:S(2)}) copy-start(f32[1536]{0:T(1024)} %copy-done.32) | copy-start | bytes 18436
  218.0 81.5 %copy-start.39 = (f32[1536]{0:T(1024)S(1)}, f32[1536]{0:T(1024)}, u32[]{:S(2)}) copy-start(f32[1536]{0:T(1024)} %copy-done.38) | copy-start | bytes 18436
  218.0 81.5 %copy-start.44 = (f32[768]{0:T(1024)S(1)}, f32[768]{0:T(1024)}, u32[]{:S(2)}) copy-start(f32[768]{0:T(1024)} %copy-done.43) | copy-start | bytes 9220
  218.0 81.5 %copy-start.51 = (f32[768]{0:T(1024)S(1)}, f32[768]{0:T(1024)}, u32[]{:S(2)}) copy-start(f32[768]{0:T(1024)} %get-tuple-element.119) | copy-start | bytes 9220
  304.8 2.2 copy-start.3
  304.8 4.4 copy-start.29
  309.1 10.1 %copy-start.40 = (f32[3,80]{1,0:T(4,128)}, f32[3,80]{1,0:T(4,128)S(1)}, u32[]{:S(2)}) copy-start(f32[3,80]{1,0:T(4,128)S(1)} %broadcast_multiply_fusion.7) | copy-start | bytes 2884
  311.3 7.9 copy-start.45
  311.3 7.9 copy-start.46
  312.8 6.4 copy-start.47
  314.4 4.8 copy-start.16
  314.4 5.5 copy-start.9
  321.4 142.6 %reduce-scatter.5.cloned.1.call-start = ((), (), s32[]{:S(2)}) async-start(), calls=%async_computation.7 | async-start | bytes 2654208 | tf_op jit(solution)/shard_map/reduce_scatter | solution.py:240
  355.9 4.6 copy-start.7
  355.9 6.3 copy-start.18
  361.3 0.9 copy-start.4
  364.9 2.7 copy-start.11
  364.9 2.7 copy-start.15
  364.9 2.7 copy-start.28
  367.5 0.9 copy-start.27
  367.6 2.0 copy-start.12
  394.6 141.3 %reduce-scatter.9.cloned.1.call-start = ((), (), s32[]{:S(2)}) async-start(), calls=%async_computation.10 | async-start | bytes 2654208 | tf_op jit(solution)/shard_map/reduce_scatter | solution.py:240
  397.6 209.7 %reduce-scatter.11.cloned.1.call-start = ((), (), s32[]{:S(2)}) async-start(), calls=%async_computation.12 | async-start | bytes 2654208 | tf_op jit(solution)/shard_map/reduce_scatter | solution.py:240
  402.4 271.2 %reduce-scatter.7.cloned.1.call-start = ((), (), s32[]{:S(2)}) async-start(), calls=%async_computation.9 | async-start | bytes 884736 | tf_op jit(solution)/shard_map/reduce_scatter | solution.py:240
  406.2 362.0 %all-reduce.9.cloned.1.call-start = ((), (), s32[]{:S(2)}) async-start(), calls=%async_computation.6 | async-start | bytes 9437184 | tf_op jit(solution)/shard_map/psum | solution.py:212
  412.7 131.1 %copy-start.41 = (f32[3,80]{1,0:T(4,128)S(1)}, f32[3,80]{1,0:T(4,128)}, u32[]{:S(2)}) copy-start(f32[3,80]{1,0:T(4,128)} %copy-done.40) | copy-start | bytes 2884
  412.7 410.6 %all-gather.6.cloned.1.call-start = ((), (), s32[]{:S(2)}) async-start(), calls=%async_computation.8 | async-start | bytes 2654208 | tf_op jit(solution)/shard_map/all_gather | solution.py:262
  466.2 410.0 %all-gather.8.cloned.1.call-start = ((), (), s32[]{:S(2)}) async-start(), calls=%async_computation.11 | async-start | bytes 2654208 | tf_op jit(solution)/shard_map/all_gather | solution.py:264
  538.2 391.2 %all-gather.10.cloned.1.call-start = ((), (), s32[]{:S(2)}) async-start(), calls=%async_computation.13 | async-start | bytes 2654208 | tf_op jit(solution)/shard_map/all_gather | solution.py:265
  550.1 60.1 %copy-start.49 = (f32[768]{0:T(1024)S(1)}, f32[768]{0:T(1024)}, u32[]{:S(2)}) copy-start(f32[768]{0:T(1024)} %get-tuple-element.65) | copy-start | bytes 9220
  550.2 63.4 %copy-start.48 = (f32[768]{0:T(1024)S(1)}, f32[768]{0:T(1024)}, u32[]{:S(2)}) copy-start(f32[768]{0:T(1024)} %get-tuple-element.66) | copy-start | bytes 9220
  550.2 113.1 %copy-start.37 = (f32[6,768]{1,0:T(8,128)S(1)}, f32[6,768]{1,0:T(8,128)}, u32[]{:S(2)}) copy-start(f32[6,768]{1,0:T(8,128)} %param.33) | copy-start | bytes 55300
  550.2 119.1 %copy-start.5 = (f32[240,768]{1,0:T(8,128)S(1)}, f32[240,768]{1,0:T(8,128)}, u32[]{:S(2)}) copy-start(f32[240,768]{1,0:T(8,128)} %copy-done.4) | copy-start | bytes 2211844
  550.2 119.1 %copy-start.35 = (pred[3,512]{1,0:T(4,128)(4,1)S(1)}, pred[3,512]{1,0:T(4,128)(4,1)}, u32[]{:S(2)}) copy-start(pred[3,512]{1,0:T(4,128)(4,1)} %copy-done.34) | copy-start | bytes 4612
  613.6 6.5 copy-start.42
  710.3 65.4 %copy-start.21 = (f32[1,96,768]{2,1,0:T(8,128)S(1)}, f32[1,96,768]{2,1,0:T(8,128)}, u32[]{:S(2)}) copy-start(f32[1,96,768]{2,1,0:T(8,128)} %get-tuple-element.100) | copy-start | bytes 884740
  710.3 66.3 %copy-start.22 = (f32[1,96,768]{2,1,0:T(8,128)S(1)}, f32[1,96,768]{2,1,0:T(8,128)}, u32[]{:S(2)}) copy-start(f32[1,96,768]{2,1,0:T(8,128)} %get-tuple-element.96) | copy-start | bytes 884740
  768.2 6.6 copy-start.24
  768.2 6.6 copy-start.25
  768.2 8.3 copy-start.23
  929.3 3.4 copy-start.19
  (1 other events, 0.7 us)
Sparse Core Ops, SparseCore 0:
  46.3 122.7 all-gather.11
  205.4 94.0 all-reduce.4
  321.5 34.3 all-reduce.6
  394.7 69.1 reduce-scatter.4
  467.9 67.9 reduce-scatter.8
  539.2 67.9 reduce-scatter.10
  611.2 61.4 reduce-scatter.6
  675.2 93.0 all-reduce.8
  771.2 52.0 all-gather.5
  825.6 50.5 all-gather.7
  878.7 50.5 all-gather.9
